TPU v7x, 256 devices: a whole 4x4x8 slice. The times are simulated.
256 devices in a mesh: img: 64 (over z, y, x_lo), txt: 4 (over x_hi, core).
Axes of the slice: x: 4 (x_hi: 2, x_lo: 2; x = x_hi * 2 + x_lo), y: 4, z: 8, core: 2. Of those that a mesh axis runs over, the one named last changes fastest.
Arguments:
- picture_vector_matrix: bfloat16 [65536, 1152], P(('img', 'txt')), may hold values from -1 to 1
- caption_vector_matrix: bfloat16 [65536, 1152], P(('img', 'txt')), may hold values from -1 to 1
- matched_caption_position: int32 [65536], P(('img', 'txt')), may hold values from 0 to 65535, as said below
- sharpness_factor: float32 [1], replicated, may hold values from 1 to 3
- pairwise_score_shift: float32 [1], replicated, may hold values from -3 to -1
Outputs:
- loss_rows: float32 [65536], P(('img', 'txt'))
- grad_images: float32 [65536, 1152], P(('img', 'txt'))
- text_embedding_gradient: float32 [65536, 1152], P(('img', 'txt'))
Inputs may be any that keep to these rules, and one draw needn't show every extreme that they name: `matched_caption_position`: image rows g*1024 to (g+1)*1024 - 1 are paired one to one with the text rows of the same range, for every group g.
All inputs are finite; a program needn't handle non-finite values.
Results may differ from a plain program's by a relative error of at most 0.002.
Values may be sent and summed in bfloat16 or wider, within the bound.
A program may use at most 128 MiB of HBM per device.

v0:
```python
import jax
import jax.numpy as jnp
from jax import lax
from jax.sharding import PartitionSpec as P

STEPS = 4


def passed_along(block, axis, distance):
    devices = range(lax.axis_size(axis))
    route = [((i - distance) % len(devices), i) for i in devices]
    return lax.ppermute(block, axis, route)


def body(
    picture_vector_matrix,
    caption_vector_matrix,
    matched_caption_position,
    sharpness_factor,
    pairwise_score_shift,
):
    score_multiplier = sharpness_factor[0]
    displacement = pairwise_score_shift[0]
    rows = picture_vector_matrix.shape[0]
    group_rows_count = rows * lax.axis_size("txt")
    my_group = lax.axis_index("img")
    objective_aggregate = jnp.zeros((rows,), jnp.float32)
    picture_aggregate = jnp.zeros(picture_vector_matrix.shape, jnp.float32)
    caption_derivative = None
    block_acc = None
    caption_tile = lax.all_gather(caption_vector_matrix, "txt", axis=0, tiled=True)
    for rotation in range(STEPS):
        if rotation > 0:
            caption_tile = passed_along(caption_tile, "img", 1)
        similarity_matrix = lax.dot_general(
            picture_vector_matrix,
            caption_tile,
            (((1,), (1,)), ((), ())),
            preferred_element_type=jnp.float32,
        )
        pairwise_scores = score_multiplier * similarity_matrix + displacement
        if rotation == 0:
            columns = my_group * group_rows_count + jnp.arange(group_rows_count, dtype=jnp.int32)
            labels = (matched_caption_position[:, None] == columns[None, :]).astype(jnp.float32)
            objective_aggregate = jnp.sum(
                jax.nn.softplus(-(2.0 * labels - 1.0) * pairwise_scores), axis=1
            )
            derivative = (jax.nn.sigmoid(pairwise_scores) - labels).astype(jnp.bfloat16)
        else:
            objective_aggregate = objective_aggregate + jnp.sum(
                jax.nn.softplus(pairwise_scores), axis=1
            )
            derivative = jax.nn.sigmoid(pairwise_scores).astype(jnp.bfloat16)
        picture_aggregate = picture_aggregate + jnp.dot(
            derivative, caption_tile, preferred_element_type=jnp.float32
        )
        summand = score_multiplier * lax.dot_general(
            derivative,
            picture_vector_matrix,
            (((0,), (0,)), ((), ())),
            preferred_element_type=jnp.float32,
        )
        if rotation == 0:
            block_acc = summand
        else:
            block_acc = passed_along(block_acc, "img", 1) + summand
    summed = lax.psum_scatter(block_acc, "txt", scatter_dimension=0, tiled=True)
    caption_derivative = passed_along(summed, "img", -(STEPS - 1))
    return (objective_aggregate, score_multiplier * picture_aggregate, caption_derivative)


def solution(mesh):
    return jax.shard_map(
        body,
        mesh=mesh,
        in_specs=(P(("img", "txt"), None), P(("img", "txt"), None), P(("img", "txt")), P(), P()),
        out_specs=(P(("img", "txt")), P(("img", "txt"), None), P(("img", "txt"), None)),
        check_vma=False,
    )
```

profile of v0, /device:TPU:1, one launch (start us, length us, event | category | flops | bytes accessed | tf_op | source)
XLA Modules:
  0.0 627.6 jit_solution(1457228933302032815)
XLA Ops:
  7.2 0.7 all-gather.2.cloned.1.call-update
  9.3 35.5 %all-gather.2.cloned.1.call-done = bf16[1024,1152]{1,0:T(8,128)(2,1)} async-done(((bf16[256,1152]{1,0:T(8,128)(2,1)}), bf16[1024,1152]{1,0:T(8,128)(2,1)}) %all-gather.2.cloned.1.call-update) | async-done | bytes 2359312 | tf_op jit(solution)/shard_map/all_gather | solution.py:31
  44.7 3.2 fusion.11
  48.0 1.1 convolution_multiply_fusion.3
  49.0 0.4 collective-permute-start.3
  49.4 0.6 copy-done.1
  50.0 1.5 collective-permute-start
  51.5 155.5 %collective-permute-done = bf16[1024,1152]{1,0:T(8,128)(2,1)S(1)} collective-permute-done((bf16[1024,1152]{1,0:T(8,128)(2,1)S(1)}, bf16[1024,1152]{1,0:T(8,128)(2,1)S(1)}, u32[]{:S(2)}, u32[]{:S(2)}) %collective-permute-start) | collective-permute-done | bytes 2359328 | tf_op jit(solution)/shard_map/ppermute | solution.py:12
  207.0 1.3 fusion.12
  208.3 1.0 fusion
  209.4 0.1 collective-permute-start.4
  209.6 156.9 %collective-permute-done.1 = bf16[1024,1152]{1,0:T(8,128)(2,1)S(1)} collective-permute-done((bf16[1024,1152]{1,0:T(8,128)(2,1)S(1)}, bf16[1024,1152]{1,0:T(8,128)(2,1)S(1)}, u32[]{:S(2)}, u32[]{:S(2)}) %collective-permute-start.1) | collective-permute-done | bytes 2359328 | tf_op jit(solution)/shard_map/ppermute | solution.py:12
  366.4 1.3 fusion.13
  367.8 1.0 convolution_multiply_fusion.1
  368.8 0.5 add.105
  369.4 0.3 collective-permute-start.2
  369.7 155.8 %collective-permute-done.2 = bf16[1024,1152]{1,0:T(8,128)(2,1)S(1)} collective-permute-done((bf16[1024,1152]{1,0:T(8,128)(2,1)S(1)}, bf16[1024,1152]{1,0:T(8,128)(2,1)S(1)}, u32[]{:S(2)}, u32[]{:S(2)}) %collective-permute-start.2) | collective-permute-done | bytes 2359328 | tf_op jit(solution)/shard_map/ppermute | solution.py:12
  525.4 1.3 fusion.14
  526.8 0.1 copy-done.5
  526.9 1.0 convolution_multiply_fusion
  528.0 2.6 add.106
  530.6 3.9 fusion.16
  534.5 54.8 %reduce-scatter.2.cloned.1.call-done = f32[256,1152]{1,0:T(8,128)} async-done(((f32[1024,1152]{1,0:T(8,128)}), f32[256,1152]{1,0:T(8,128)}) %reduce-scatter.2.cloned.1.call-update) | async-done | bytes 1179664 | tf_op jit(solution)/shard_map/reduce_scatter | solution.py:67
  589.3 5.5 collective-permute-start.6
  594.8 2.8 convolution_add_fusion.2
  597.7 0.9 convolution_add_fusion.1
  598.6 0.6 add_add_fusion
  599.2 0.2 copy-done.6
  599.3 0.3 copy-done.9
  599.6 1.9 fusion.1
  601.5 18.3 %collective-permute-done.6 = f32[256,1152]{1,0:T(8,128)S(1)} collective-permute-done((f32[256,1152]{1,0:T(8,128)}, f32[256,1152]{1,0:T(8,128)S(1)}, u32[]{:S(2)}, u32[]{:S(2)}) %collective-permute-start.6) | collective-permute-done | bytes 1179680 | tf_op jit(solution)/shard_map/ppermute | solution.py:12
  619.8 1.0 copy.11
  (27 shorter events, 0.3 us)
Async XLA Ops:
  7.2 37.6 %copy-start = (bf16[256,1152]{1,0:T(8,128)(2,1)S(1)}, bf16[256,1152]{1,0:T(8,128)(2,1)}, u32[]{:S(2)}) copy-start(bf16[256,1152]{1,0:T(8,128)(2,1)} %param.5) | copy-start | bytes 1769476
  7.2 37.5 %all-gather.2.cloned.1.call-start = ((), (), s32[]{:S(2)}) async-start(), calls=%async_computation.1 | async-start | bytes 2949120 | tf_op jit(solution)/shard_map/all_gather | solution.py:31
  7.9 581.4 %reduce-scatter.2.cloned.1.call-start = ((), (), s32[]{:S(2)}) async-start(), calls=%async_computation.2 | async-start | bytes 5898240 | tf_op jit(solution)/shard_map/reduce_scatter | solution.py:67
  44.7 3.2 copy-start.7
  47.9 1.1 copy-start.10
  47.9 2.0 copy-start.1
  49.0 159.3 %collective-permute-start.3 = (f32[1024,1152]{1,0:T(8,128)S(1)}, f32[1024,1152]{1,0:T(8,128)S(1)}, u32[]{:S(2)}, u32[]{:S(2)}) collective-permute-start(f32[1024,1152]{1,0:T(8,128)S(1)} %convolution_multiply_fusion.3), channel_id=1, source_target_pairs={{252,0},{0,4},{4,8},{8,12},{12,16},{16,20},{20,24},{24,28},{28,32}... | collective-permute-start | bytes 14155784 | tf_op jit(solution)/shard_map/ppermute | solution.py:12
  50.0 157.0 %collective-permute-start = (bf16[1024,1152]{1,0:T(8,128)(2,1)S(1)}, bf16[1024,1152]{1,0:T(8,128)(2,1)S(1)}, u32[]{:S(2)}, u32[]{:S(2)}) collective-permute-start(bf16[1024,1152]{1,0:T(8,128)(2,1)S(1)} %copy-done.1), channel_id=1, source_target_pairs={{252,0},{0,4},{4,8},{8,12},{12,16},{16,20},{20,24},{24,28},{28,32}... | collective-permute-start | bytes 7077896 | tf_op jit(solution)/shard_map/ppermute | solution.py:12
  207.0 2.5 copy-start.2
  209.4 159.4 %collective-permute-start.4 = (f32[1024,1152]{1,0:T(8,128)S(1)}, f32[1024,1152]{1,0:T(8,128)S(1)}, u32[]{:S(2)}, u32[]{:S(2)}) collective-permute-start(f32[1024,1152]{1,0:T(8,128)S(1)} %fusion), channel_id=1, source_target_pairs={{252,0},{0,4},{4,8},{8,12},{12,16},{16,20},{20,24},{24,28},{28,32}... | collective-permute-start | bytes 14155784 | tf_op jit(solution)/shard_map/ppermute | solution.py:12
  209.5 157.0 %collective-permute-start.1 = (bf16[1024,1152]{1,0:T(8,128)(2,1)S(1)}, bf16[1024,1152]{1,0:T(8,128)(2,1)S(1)}, u32[]{:S(2)}, u32[]{:S(2)}) collective-permute-start(bf16[1024,1152]{1,0:T(8,128)(2,1)S(1)} %collective-permute-done), channel_id=1, source_target_pairs={{252,0},{0,4},{4,8},{8,12},{12,16},{16,20},{20,24},{24,28},{28,32}... | collective-permute-start | bytes 7077896 | tf_op jit(solution)/shard_map/ppermute | solution.py:12
  366.4 3.0 copy-start.3
  369.3 158.6 %collective-permute-start.5 = (f32[1024,1152]{1,0:T(8,128)S(1)}, f32[1024,1152]{1,0:T(8,128)S(1)}, u32[]{:S(2)}, u32[]{:S(2)}) collective-permute-start(f32[1024,1152]{1,0:T(8,128)S(1)} %add.105), channel_id=1, source_target_pairs={{252,0},{0,4},{4,8},{8,12},{12,16},{16,20},{20,24},{24,28},{28,32}... | collective-permute-start | bytes 14155784 | tf_op jit(solution)/shard_map/ppermute | solution.py:12
  369.4 156.0 %collective-permute-start.2 = (bf16[1024,1152]{1,0:T(8,128)(2,1)S(1)}, bf16[1024,1152]{1,0:T(8,128)(2,1)S(1)}, u32[]{:S(2)}, u32[]{:S(2)}) collective-permute-start(bf16[1024,1152]{1,0:T(8,128)(2,1)S(1)} %collective-permute-done.1), channel_id=1, source_target_pairs={{252,0},{0,4},{4,8},{8,12},{12,16},{16,20},{20,24},{24,28},{28,32}... | collective-permute-start | bytes 7077896 | tf_op jit(solution)/shard_map/ppermute | solution.py:12
  525.4 1.5 copy-start.5
  526.9 1.0 copy-start.8
  589.3 8.4 %copy-start.4 = (bf16[1024,1152]{1,0:T(8,128)(2,1)S(1)}, bf16[1024,1152]{1,0:T(8,128)(2,1)}, u32[]{:S(2)}) copy-start(bf16[1024,1152]{1,0:T(8,128)(2,1)} %copy-done.3) | copy-start | bytes 7077892
  589.3 30.4 %collective-permute-start.6 = (f32[256,1152]{1,0:T(8,128)}, f32[256,1152]{1,0:T(8,128)S(1)}, u32[]{:S(2)}, u32[]{:S(2)}) collective-permute-start(f32[256,1152]{1,0:T(8,128)} %reduce-scatter.2.cloned.1.call-done), channel_id=1, source_target_pairs={{12,0},{16,4},{20,8},{24,12},{28,16},{32,20},{36,24},{40,28},{44,3... | collective-permute-start | bytes 3538952 | tf_op jit(solution)/shard_map/ppermute | solution.py:12
  597.7 1.7 copy-start.6
  597.7 1.9 copy-start.9
Sparse Core Ops, SparseCore 0:
  9.8 34.8 all-gather.1
  530.7 58.5 reduce-scatter.1
where the time goes:
time: 628 us
  waiting for transfers between devices  577 us (92%)
  matrix products  20.9 us (3%)
  between operations  15.5 us (2%)
  starting transfers between devices  7.96 us (1%)
    ppermute x7, waiting for transfers between devices, passed_along(): return lax.ppermute(block, axis, route)  486 us
    reduce_scatter x1, waiting for transfers between devices, body(): summed = lax.psum_scatter(block_acc, 'txt', scatter_dimension=0, tiled=True)  54.8 us
    all_gather x1, waiting for transfers between devices, body(): lax.all_gather(caption_vector_matrix, 'txt', axis=0, tiled=True)  35.5 us
  transfers between devices with their start and end apart: 9, of which 6 were waited for; matrix products, arithmetic and copies ran while one was open for 3% of the time, Pallas kernels for 0%

commit v1 on v0

v1 whole, which is shorter than its diff:
```python
import functools

import jax
import jax.numpy as jnp
from jax import lax
from jax.experimental import pallas as pl
from jax.experimental.pallas import tpu as pltpu
from jax.sharding import PartitionSpec as P

MESH = pl.DeviceIdType.MESH
D = 1152
B = 256
HALF = 128
H = 2
SR = B // H
TR = 2 * SR
TILES = 3 * H
NIMG = 64
LN2_SERIES_LIMIT = 2.0**-6


def kernel(
    pic, cap, mat, sc, sh, loss_o, di_o, dt_o,
    img, txt, wt, wn, matm, lacc, lrecv, pi, pt, rcc,
    sx_dir, rx_dir, sx_rel, rx_rel, sy_q, ry_q,
    lsem, ag_s, ag_r, fw_s, fw_r, ty_s, ty_r, tc_s, tc_r, m_s, m_r,
    dir_s, dir_r, rel_s, rel_r, q_s, q_r, ex_s, ex_r, l_s, l_r,
):
    gi = lax.axis_index("img")
    ti = lax.axis_index("txt")
    row2 = (gi // 2) * 2
    xlo = gi % 2
    xhi = ti // 2
    core = ti % 2
    other = 1 - core
    odd = xlo == 1
    even = xlo == 0

    x_up = (row2 + 1 - xlo, ((xhi + xlo) % 2) * 2 + core)
    x_dn = (row2 + 1 - xlo, ((xhi + 1 - xlo) % 2) * 2 + core)
    x_far = (gi, (1 - xhi) * 2 + core)
    y_up = ((gi + 2) % NIMG, ti)
    y_dn = ((gi + NIMG - 2) % NIMG, ti)
    sib = (gi, xhi * 2 + other)

    scale = sc[0]
    shift = sh[0]

    barrier = pltpu.get_barrier_semaphore()
    for dev in (x_up, x_dn, x_far, y_up, y_dn, sib):
        pl.semaphore_signal(barrier, inc=1, device_id=dev, device_id_type=MESH)

    own_img = pltpu.make_async_copy(pic, img.at[pl.ds(0, B)], lsem.at[0])
    own_img.start()
    own_txt = []
    for h in range(H):
        own_txt.append(
            pltpu.make_async_copy(cap.at[h], txt.at[pl.ds(text_row(0, h, core), SR)], lsem.at[1 + h])
        )
        own_txt[h].start()
    matm[0] = jnp.broadcast_to(mat[...], (8, B))
    lacc[...] = jnp.zeros_like(lacc)
    pl.semaphore_wait(barrier, 6)

    def remote(src, dst, s, r, dev):
        return pltpu.make_async_remote_copy(
            src_ref=src, dst_ref=dst, send_sem=s, recv_sem=r, device_id=dev, device_id_type=MESH
        )

    def ag(d, half):
        rows = pl.ds(half * HALF, HALF)
        to_pos = 3 - d
        return remote(
            pic.at[rows], img.at[pl.ds(to_pos * B + half * HALF, HALF)],
            ag_s.at[d, half], ag_r.at[d, half], x_up if d == 0 else x_dn,
        )

    def fw(d):
        return remote(
            img.at[pl.ds((3 - d) * B + d * HALF, HALF)], img.at[pl.ds(B + d * HALF, HALF)],
            fw_s.at[d], fw_r.at[d], x_up if d == 0 else x_dn,
        )

    def ty(s, h):
        dst = txt.at[pl.ds(text_row(s, h, core), SR)]
        src = cap.at[h] if s == 1 else txt.at[pl.ds(text_row(s - 1, h, core), SR)]
        return remote(src, dst, ty_s.at[s - 1, h], ty_r.at[s - 1, h], y_up)

    def tc(s, h, receive=False):
        src = cap.at[h] if s == 0 else txt.at[pl.ds(text_row(s, h, core), SR)]
        dst = txt.at[pl.ds(text_row(s, h, other if receive else core), SR)]
        return remote(src, dst, tc_s.at[s, h], tc_r.at[s, h], sib)

    for d, half in ((0, 0), (1, 1), (0, 1), (1, 0)):
        ag(d, half).start()
    ty(1, 0).start()

    @pl.when(even)
    def _():
        for h in range(1, H):
            ty(1, h).start()

    for h in range(H):
        tc(0, h).start()
    far_match = remote(matm.at[0], matm.at[1], m_s, m_r, x_far)
    far_match.start()

    text_base = gi * 1024 + xhi * 512

    def scores(tile, pos):
        rows = pl.ds(pl.multiple_of(tile * TR, TR), TR)
        images = pl.ds(pl.multiple_of(pos * B, B), B)
        sims = lax.dot_general(
            txt[rows, :], img[images, :], (((1,), (1,)), ((), ())), preferred_element_type=jnp.float32
        )
        x = scale * sims + shift
        i = lax.broadcasted_iota(jnp.int32, (TR, 1), 0)
        ids = text_base + (i // SR) * B + (i % SR)
        has_label = jnp.logical_and(tile < H, pos < 2)
        ids = ids + jnp.where(has_label, tile * SR, -(1 << 30))
        label = ids == matm[jnp.minimum(pos, 1), 0:1, :]
        e = jnp.exp(-jnp.abs(x))
        u = 1.0 + e
        big = 1.0 / u
        small = e * big
        positive = x >= 0.0
        w = jnp.where(jnp.logical_xor(positive, label), big, small)
        w = jnp.where(label, -w, w).astype(jnp.bfloat16)
        series = e * (1.0 - e * (0.5 - e * (1.0 / 3.0)))
        lp = jnp.where(e < LN2_SERIES_LIMIT, series, jnp.log(u))
        loss = lp + jnp.maximum(jnp.where(label, -x, x), 0.0)
        wt[rows, images] = w
        wn[images, rows] = w.T
        lacc[pos] += jnp.sum(loss.reshape(TR // 8, 8, B), axis=0)

    def scores_loop(n, tile_of, pos_of):
        @pl.loop(0, n)
        def _(j):
            scores(tile_of(j), pos_of(j))

    def image_part(pos, base):
        cols = pl.ds(base * TR, 2 * B * 2)
        pi[pl.ds(pos * B, B)] = jnp.dot(
            wn[pl.ds(pos * B, B), cols], txt[cols, :], preferred_element_type=jnp.float32
        )

    def text_part(tile, first, count):
        rows = pl.ds(tile * TR, TR)
        ks = pl.ds(first * B, count * B)
        pt[rows] = jnp.dot(wt[rows, ks], img[ks, :], preferred_element_type=jnp.float32)

    def ex(s, h):
        tile = s * H + h
        return remote(
            pt.at[pl.ds(text_row(s, h, other), SR)], rcc.at[pl.ds(tile * SR, SR)],
            ex_s.at[s, h], ex_r.at[s, h], sib,
        )

    def chip_sum(s, h):
        tile = s * H + h
        ex(s, h).wait_recv()
        return pt[pl.ds(text_row(s, h, core), SR), :] + rcc[pl.ds(tile * SR, SR), :]

    def q(s, h):
        rows = pl.ds(((s - 1) * H + h) * SR, SR)
        return remote(sy_q.at[rows], ry_q.at[rows], q_s.at[s - 1, h], q_r.at[s - 1, h], y_dn)

    def q_send(s, h, chain=False):
        value = chip_sum(s, h)
        rows = pl.ds(((s - 1) * H + h) * SR, SR)
        if chain:
            q(2, h).wait_recv()
            value = value + ry_q[pl.ds((H + h) * SR, SR), :].astype(jnp.float32)
        sy_q[rows, :] = value.astype(jnp.bfloat16)
        q(s, h).start()

    def rel(d):
        rows = pl.ds(d * HALF, HALF)
        return remote(
            sx_rel.at[rows], rx_rel.at[rows], rel_s.at[d], rel_r.at[d], x_up if d == 0 else x_dn
        )

    def rel_send():
        sx_rel[...] = pi[pl.ds(B, B), :].astype(jnp.bfloat16)
        rel(0).start()
        rel(1).start()

    def direct(d, half):
        rows = pl.ds(d * B + half * HALF, HALF)
        return remote(
            sx_dir.at[rows], rx_dir.at[rows], dir_s.at[d, half], dir_r.at[d, half],
            x_up if d == 0 else x_dn,
        )

    def direct_send(d, half, relayed):
        rows = pl.ds(d * B + half * HALF, HALF)
        value = pi[pl.ds((2 + d) * B + half * HALF, HALF), :]
        if relayed:
            rel(d).wait_recv()
            value = value + rx_rel[pl.ds(d * HALF, HALF), :].astype(jnp.float32)
        sx_dir[rows, :] = value.astype(jnp.bfloat16)
        direct(d, half).start()

    def loss_copy(pos):
        dev = {1: x_far, 2: x_up, 3: x_dn}[pos]
        return remote(lacc.at[pos], lrecv.at[pos - 1], l_s.at[pos - 1], l_r.at[pos - 1], dev)

    def arrive(s, h):
        ty(s, h).wait_recv()
        tc(s, h).start()

    def arrive_sib(s, h):
        tc(s, h, receive=True).wait_recv()

    own_img.wait()
    for h in range(H):
        own_txt[h].wait()
    for h in range(H):
        tc(0, h, receive=True).wait_recv()
    far_match.wait_recv()
    scores_loop(H, lambda j: j, lambda j: 0)

    arrive(1, 0)

    @pl.when(odd)
    def _():
        ty(2, 0).start()
        ty(1, 1).start()

    arrive_sib(1, 0)
    scores_loop(1, lambda j: j + H, lambda j: 0)

    for d in range(2):
        for half in range(2):
            ag(d, half).wait_recv()
    fw(0).start()
    fw(1).start()

    @pl.when(even)
    def _():
        arrive(1, 1)
        scores_loop(4, lambda j: j % 2, lambda j: 2 + j // 2)
        arrive_sib(1, 1)
        scores_loop(4, lambda j: 2 + j % 2, lambda j: 2 + j // 2)
        image_part(2, 0)
        direct_send(0, 1, False)
        image_part(3, 0)
        direct_send(1, 0, False)
        scores_loop(1, lambda j: j + 3, lambda j: 0)
        fw(0).wait_recv()
        fw(1).wait_recv()
        scores_loop(4, lambda j: j, lambda j: 1)
        image_part(1, 0)
        rel_send()
        for h in range(H):
            text_part(H + h, 0, 4)
            ex(1, h).start()
        for h in range(H):
            q_send(1, h)
        for pos in (1, 2, 3):
            loss_copy(pos).start()
        for h in range(H):
            text_part(h, 0, 4)
            ex(0, h).start()
        image_part(0, 0)
        direct_send(0, 0, True)
        direct_send(1, 1, True)

    @pl.when(odd)
    def _():
        arrive(2, 0)
        scores_loop(2, lambda j: j + 2 - j, lambda j: 2 + j)
        arrive_sib(2, 0)
        scores_loop(2, lambda j: j + 4 - j, lambda j: 2 + j)
        text_part(2 * H, 2, 2)
        ex(2, 0).start()
        arrive(1, 1)
        ty(2, 1).start()
        q_send(2, 0)
        arrive_sib(1, 1)
        scores_loop(3, lambda j: j + 3 - j, lambda j: jnp.where(j == 0, 0, j + 1))
        fw(0).wait_recv()
        fw(1).wait_recv()
        scores_loop(4, lambda j: j, lambda j: 1)
        image_part(1, 0)
        rel_send()
        for h in range(H):
            text_part(H + h, 0, 4)
            ex(1, h).start()
        q_send(1, 0, chain=True)
        arrive(2, 1)
        arrive_sib(2, 1)
        scores_loop(2, lambda j: j + 5 - j, lambda j: 2 + j)
        text_part(2 * H + 1, 2, 2)
        ex(2, 1).start()
        image_part(2, H)
        direct_send(0, 1, False)
        q_send(2, 1)
        image_part(3, H)
        direct_send(1, 0, False)
        for pos in (1, 2, 3):
            loss_copy(pos).start()
        direct_send(0, 0, True)
        direct_send(1, 1, True)
        for h in range(H):
            text_part(h, 0, 2)
            ex(0, h).start()
        image_part(0, 0)
        q_send(1, 1, chain=True)

    total = lacc[0]
    for pos in (1, 2, 3):
        loss_copy(pos).wait_recv()
        total = total + lrecv[pos - 1]
    loss_o[...] = jnp.sum(total, axis=0, keepdims=True)
    for d, half in ((0, 1), (1, 0), (0, 0), (1, 1)):
        direct(d, half).wait_recv()
    di_o[...] = scale * (
        pi[pl.ds(0, B), :]
        + rx_dir[pl.ds(0, B), :].astype(jnp.float32)
        + rx_dir[pl.ds(B, B), :].astype(jnp.float32)
    )
    for h in range(H):
        own = chip_sum(0, h)
        q(1, h).wait_recv()
        dt_o[pl.ds(h * SR, SR), :] = scale * (own + ry_q[pl.ds(h * SR, SR), :].astype(jnp.float32))

    for d in range(2):
        fw(d).wait_send()
        rel(d).wait_send()
        for half in range(2):
            ag(d, half).wait_send()
            direct(d, half).wait_send()
    for h in range(H):
        ty(1, h).wait_send()
        tc(0, h).wait_send()
        tc(1, h).wait_send()
        ex(0, h).wait_send()
        ex(1, h).wait_send()
        q(1, h).wait_send()
    far_match.wait_send()
    for pos in (1, 2, 3):
        loss_copy(pos).wait_send()

    @pl.when(odd)
    def _():
        for h in range(H):
            ty(2, h).wait_send()
            tc(2, h).wait_send()
            ex(2, h).wait_send()
            q(2, h).wait_send()


def text_row(s, h, core):
    return pl.multiple_of(((s * H + h) * 2 + core) * SR, SR)


def body(pic, cap, mat, sc, sh):
    any_spec = pl.BlockSpec(memory_space=pl.ANY)
    vmem = pl.BlockSpec(memory_space=pltpu.VMEM)
    smem = pl.BlockSpec(memory_space=pltpu.SMEM)
    f32, bf16 = jnp.float32, jnp.bfloat16
    dma = pltpu.SemaphoreType.DMA
    loss, di, dt = pl.pallas_call(
        kernel,
        name="band",
        out_shape=(
            jax.ShapeDtypeStruct((1, B), f32),
            jax.ShapeDtypeStruct((B, D), f32),
            jax.ShapeDtypeStruct((B, D), f32),
        ),
        in_specs=[any_spec, any_spec, vmem, smem, smem],
        out_specs=(vmem, vmem, vmem),
        scratch_shapes=[
            pltpu.VMEM((4 * B, D), bf16),
            pltpu.VMEM((TILES * TR, D), bf16),
            pltpu.VMEM((TILES * TR, 4 * B), bf16),
            pltpu.VMEM((4 * B, TILES * TR), bf16),
            pltpu.VMEM((2, 8, B), jnp.int32),
            pltpu.VMEM((4, 8, B), f32),
            pltpu.VMEM((3, 8, B), f32),
            pltpu.VMEM((4 * B, D), f32),
            pltpu.VMEM((TILES * TR, D), f32),
            pltpu.VMEM((TILES * SR, D), f32),
            pltpu.VMEM((2 * B, D), bf16),
            pltpu.VMEM((2 * B, D), bf16),
            pltpu.VMEM((B, D), bf16),
            pltpu.VMEM((B, D), bf16),
            pltpu.VMEM((2 * B, D), bf16),
            pltpu.VMEM((2 * B, D), bf16),
            dma((1 + H,)),
            dma((2, 2)), dma((2, 2)),
            dma((2,)), dma((2,)),
            dma((2, H)), dma((2, H)),
            dma((3, H)), dma((3, H)),
            dma, dma,
            dma((2, 2)), dma((2, 2)),
            dma((2,)), dma((2,)),
            dma((2, H)), dma((2, H)),
            dma((3, H)), dma((3, H)),
            dma((3,)), dma((3,)),
        ],
        compiler_params=pltpu.CompilerParams(
            collective_id=0, has_side_effects=True, vmem_limit_bytes=56 * 2**20
        ),
        cost_estimate=pl.CostEstimate(flops=7247757312, bytes_accessed=3600000, transcendentals=3145728),
    )(pic, cap.reshape(H, SR, D), mat.reshape(1, B), sc, sh)
    return loss.reshape(B), di, dt


def solution(mesh):
    return jax.shard_map(
        body,
        mesh=mesh,
        in_specs=(P(("img", "txt"), None), P(("img", "txt"), None), P(("img", "txt")), P(), P()),
        out_specs=(P(("img", "txt")), P(("img", "txt"), None), P(("img", "txt"), None)),
        check_vma=False,
    )
```

time: 628 us -> 80 us (0.13)
  waiting for transfers between devices: 577 us -> 0 us
  Pallas kernels: 0 us -> 73.2 us
  matrix products: 20.9 us -> 0 us
  between operations: 15.5 us -> 1.93 us
  starting transfers between devices: 7.96 us -> 0 us
    ppermute x7 -> x0, waiting for transfers between devices: 486 us -> none  [passed_along(): return lax.ppermute(block, axis, route)]
    pallas_call x0 -> x1, Pallas kernels: none -> 73.2 us  [body(): pl.pallas_call(kernel, name='band', out_shape=(jax.ShapeDtypeStruct((1, B...]
    reduce_scatter x1 -> x0, waiting for transfers between devices: 54.8 us -> none  [body(): summed = lax.psum_scatter(block_acc, 'txt', scatter_dimension=0, tiled=True)]
    all_gather x1 -> x0, waiting for transfers between devices: 35.5 us -> none  [body(): lax.all_gather(caption_vector_matrix, 'txt', axis=0, tiled=True)]
    dot_general x12 -> x0, matrix products: 20.9 us -> none  [the longest x4 9.54 us: body(): jnp.dot(derivative, caption_tile, preferred_element_type=jnp.float32)]
    ppermute x7 -> x0, starting transfers between devices: 7.88 us -> none  [passed_along(): return lax.ppermute(block, axis, route)]
  transfers between devices with their start and end apart: 9 -> 0, of which waited for: 6 -> 0; matrix products, arithmetic and copies ran while one was open for 3% -> 0% of each run, Pallas kernels for 0% -> 0%
where the time goes in v1:
time: 80 us; the launch traced here: 79.8 us
  Pallas kernels  73.2 us (92%)
  local copies, waits for them, and re-layouts  4.71 us (6%)
  between operations  1.93 us (2%)
    pallas_call x1, Pallas kernels, body(): pl.pallas_call(kernel, name='band', out_shape=(jax.ShapeDtypeStruct((1, B...  73.2 us
    unnamed x5, local copies, waits for them, and re-layouts  4.71 us

profile of v1, /device:TPU:1, one launch (start us, length us, event | category | flops | bytes accessed | tf_op | source)
XLA Modules:
  0.0 79.8 jit_solution(13494397018515044283)
XLA Ops:
  1.9 73.2 %band.1 = (f32[1,256]{1,0:T(1,128)}, f32[256,1152]{1,0:T(8,128)}, f32[256,1152]{1,0:T(8,128)}) custom-call(bf16[256,1152]{1,0:T(8,128)(2,1)} %pic.1, bf16[2,128,1152]{2,1,0:T(8,128)(2,1)} %bitcast.4, s32[1,256]{1,0:T(1,128)} %bitcast.5, f32[1]{0:T(128)S(6)} %copy.11.sc, f32[1]{0:T(128)S(6)} %copy.12.sh), custom_call_target="tpu_custom_call" | custom-call | flops 7247757312 | bytes 3600000 | tf_op jit(solution)/shard_map/band/pallas_call | solution.py:364
  75.1 1.2 %copy.13 = f32[256]{0:T(256)} copy(f32[256]{0:T(256)} %bitcast.3) | data formatting | bytes 2048
  76.3 0.0 copy-start
  76.3 2.5 %copy.14 = f32[256,1152]{1,0:T(8,128)} copy(f32[256,1152]{1,0:T(8,128)} %get-tuple-element.13) | data formatting | bytes 2359296
  78.8 0.0 copy-done
  78.8 1.0 %copy.15 = f32[256,1152]{1,0:T(8,128)} copy(f32[256,1152]{1,0:T(8,128)S(1)} %copy-done) | data formatting | bytes 2359296
Async XLA Ops:
  76.3 2.5 %copy-start = (f32[256,1152]{1,0:T(8,128)S(1)}, f32[256,1152]{1,0:T(8,128)}, u32[]{:S(2)}) copy-start(f32[256,1152]{1,0:T(8,128)} %get-tuple-element.14) | copy-start | bytes 3538948

commit v2 on v1

v2 whole, which is shorter than its diff:
```python
import functools

import jax
import jax.numpy as jnp
from jax import lax
from jax.experimental import pallas as pl
from jax.experimental.pallas import tpu as pltpu
from jax.sharding import PartitionSpec as P

MESH = pl.DeviceIdType.MESH
D = 1152
B = 256
HALF = 128
H = 4
SR = B // H
TR = 2 * SR
TILES = 3 * H
NIMG = 64
LOG2E = 1.4426950408889634
LN2 = 0.6931471805599453
SERIES_LIMIT = 2.0**-6


def kernel(
    pic, cap, mat, sc, sh, loss_o, pi_o, rx_late, q0_o, ry_o,
    scal, img, txt, wt, wn, matm, lacc, lrecv, pi, pt, rcc,
    sx_dir, rx_pure, sx_rel, rx_rel, sy_q, ry_q2,
    lsem, ag_s, ag_r, fw_s, fw_r, ty_s, ty_r, tc_s, tc_r, m_s, m_r,
    dir_s, dir_r, rel_s, rel_r, q_s, q_r, ex_s, ex_r, l_s, l_r, o_s,
):
    gi = lax.axis_index("img")
    ti = lax.axis_index("txt")
    row2 = (gi // 2) * 2
    xlo = gi % 2
    xhi = ti // 2
    core = ti % 2
    other = 1 - core
    odd = xlo == 1
    even = xlo == 0

    x_up = (row2 + 1 - xlo, ((xhi + xlo) % 2) * 2 + core)
    x_dn = (row2 + 1 - xlo, ((xhi + 1 - xlo) % 2) * 2 + core)
    x_far = (gi, (1 - xhi) * 2 + core)
    y_up = ((gi + 2) % NIMG, ti)
    y_dn = ((gi + NIMG - 2) % NIMG, ti)
    sib = (gi, xhi * 2 + other)

    barrier = pltpu.get_barrier_semaphore()
    for dev in (x_up, x_dn, x_far, y_up, y_dn, sib):
        pl.semaphore_signal(barrier, inc=1, device_id=dev, device_id_type=MESH)

    own_img = pltpu.make_async_copy(pic, img.at[pl.ds(0, B)], lsem.at[0])
    own_img.start()
    own_txt = []
    for h in range(H):
        own_txt.append(
            pltpu.make_async_copy(cap.at[h], txt.at[pl.ds(text_row(0, h, core), SR)], lsem.at[1 + h])
        )
        own_txt[h].start()
    small = [
        pltpu.make_async_copy(sc, scal.at[0], lsem.at[1 + H]),
        pltpu.make_async_copy(sh, scal.at[1], lsem.at[2 + H]),
        pltpu.make_async_copy(mat, matm.at[0], lsem.at[3 + H]),
    ]
    for copy in small:
        copy.start()
    lacc[...] = jnp.zeros_like(lacc)
    pl.semaphore_wait(barrier, 6)

    def remote(src, dst, s, r, dev):
        return pltpu.make_async_remote_copy(
            src_ref=src, dst_ref=dst, send_sem=s, recv_sem=r, device_id=dev, device_id_type=MESH
        )

    def ag(d, half):
        rows = pl.ds(half * HALF, HALF)
        to_pos = 3 - d
        return remote(
            pic.at[rows], img.at[pl.ds(to_pos * B + half * HALF, HALF)],
            ag_s.at[d, half], ag_r.at[d, half], x_up if d == 0 else x_dn,
        )

    def fw(d):
        return remote(
            img.at[pl.ds((3 - d) * B + d * HALF, HALF)], img.at[pl.ds(B + d * HALF, HALF)],
            fw_s.at[d], fw_r.at[d], x_up if d == 0 else x_dn,
        )

    def ty(s, h):
        dst = txt.at[pl.ds(text_row(s, h, core), SR)]
        src = cap.at[h] if s == 1 else txt.at[pl.ds(text_row(s - 1, h, core), SR)]
        return remote(src, dst, ty_s.at[s - 1, h], ty_r.at[s - 1, h], y_up)

    def tc(s, h, receive=False):
        src = cap.at[h] if s == 0 else txt.at[pl.ds(text_row(s, h, core), SR)]
        dst = txt.at[pl.ds(text_row(s, h, other if receive else core), SR)]
        return remote(src, dst, tc_s.at[s, h], tc_r.at[s, h], sib)

    ty(1, 0).start()
    far_match = remote(mat, matm.at[1], m_s, m_r, x_far)
    far_match.start()
    for h in range(H):
        tc(0, h).start()
    ag(0, 0).start()
    ag(1, 1).start()
    ty(1, 1).start()
    ag(0, 1).start()
    ag(1, 0).start()

    @pl.when(even)
    def _():
        for h in range(2, H):
            ty(1, h).start()

    for copy in small:
        copy.wait()
    scale = scal[0, 0] * LOG2E
    shift = scal[1, 0] * LOG2E
    text_base = gi * 1024 + xhi * 512

    def scores(tile, count, pos, labelled):
        n = count * TR
        rows = pl.ds(pl.multiple_of(tile * TR, TR), n)
        images = pl.ds(pl.multiple_of(pos * B, B), B)
        sims = lax.dot_general(
            txt[rows, :], img[images, :], (((1,), (1,)), ((), ())), preferred_element_type=jnp.float32
        )
        x = scale * sims + shift
        e = jnp.exp2(-jnp.abs(x))
        u = 1.0 + e
        r = pltpu.reciprocal(u, approx=True)
        big = r * (2.0 - u * r)
        small = e * big
        series = e * (LOG2E - e * (LOG2E / 2 - e * (LOG2E / 3)))
        lp = jnp.where(e < SERIES_LIMIT, series, jnp.log2(u))
        positive = x >= 0.0
        if labelled:
            i = lax.broadcasted_iota(jnp.int32, (n, 1), 0)
            ids = text_base + ((i % TR) // SR) * B + (i // TR) * SR + i % SR
            label = ids == matm[pos]
            w = jnp.where(jnp.logical_xor(positive, label), big, small)
            w = jnp.where(label, -w, w)
            loss = lp + jnp.maximum(jnp.where(label, -x, x), 0.0)
        else:
            w = jnp.where(positive, big, small)
            loss = lp + jnp.maximum(x, 0.0)
        w = w.astype(jnp.bfloat16)
        wt[rows, images] = w
        wn[images, rows] = w.T
        lacc[pos] += jnp.sum(loss.reshape(n // 8, 8, B), axis=0)

    def scores_loop(n, tile_of, count, pos_of):
        @pl.loop(0, n)
        def _(j):
            scores(tile_of(j), count, pos_of(j), False)

    def own_scores(pos):
        scores(0, H, pos, True)

    def image_part(pos, tile, count, add=False):
        cols = pl.ds(tile * TR, count * TR)
        part = jnp.dot(wn[pl.ds(pos * B, B), cols], txt[cols, :], preferred_element_type=jnp.float32)
        if add:
            part = part + pi[pl.ds(pos * B, B)]
        pi[pl.ds(pos * B, B)] = part

    def text_part(s, h, count, first=0, blocks=4):
        rows = pl.ds((s * H + h) * TR, count * TR)
        ks = pl.ds(first * B, blocks * B)
        pt[rows] = jnp.dot(wt[rows, ks], img[ks, :], preferred_element_type=jnp.float32)
        for k in range(h, h + count):
            ex(s, k).start()

    def ex(s, h):
        tile = s * H + h
        return remote(
            pt.at[pl.ds(text_row(s, h, other), SR)], rcc.at[pl.ds(tile * SR, SR)],
            ex_s.at[s, h], ex_r.at[s, h], sib,
        )

    def chip_sum(s, h):
        tile = s * H + h
        ex(s, h).wait_recv()
        return pt[pl.ds(text_row(s, h, core), SR), :] + rcc[pl.ds(tile * SR, SR), :]

    def q(s, h):
        rows = pl.ds(h * SR, SR)
        dst = ry_o if s == 1 else ry_q2
        return remote(
            sy_q.at[pl.ds(((s - 1) * H + h) * SR, SR)], dst.at[rows], q_s.at[s - 1, h], q_r.at[s - 1, h], y_dn
        )

    def q_send(s, h, chain=False):
        value = chip_sum(s, h)
        if chain:
            q(2, h).wait_recv()
            value = value + ry_q2[pl.ds(h * SR, SR), :].astype(jnp.float32)
        sy_q[pl.ds(((s - 1) * H + h) * SR, SR), :] = value.astype(jnp.bfloat16)
        q(s, h).start()

    def rel(d):
        rows = pl.ds(d * HALF, HALF)
        return remote(
            sx_rel.at[rows], rx_rel.at[rows], rel_s.at[d], rel_r.at[d], x_up if d == 0 else x_dn
        )

    def rel_send():
        sx_rel[...] = pi[pl.ds(B, B), :].astype(jnp.bfloat16)
        rel(0).start()
        rel(1).start()

    def direct(d, half):
        rows = pl.ds(half * HALF, HALF)
        return remote(
            sx_dir.at[pl.ds(d * B + half * HALF, HALF)], (rx_late if d == half else rx_pure).at[rows],
            dir_s.at[d, half], dir_r.at[d, half], x_up if d == 0 else x_dn,
        )

    def direct_send(d, relayed):
        half = d if relayed else 1 - d
        value = pi[pl.ds((2 + d) * B + half * HALF, HALF), :]
        if relayed:
            rel(d).wait_recv()
            value = value + rx_rel[pl.ds(d * HALF, HALF), :].astype(jnp.float32)
        sx_dir[pl.ds(d * B + half * HALF, HALF), :] = value.astype(jnp.bfloat16)
        direct(d, half).start()

    def loss_copy(pos):
        dev = {1: x_far, 2: x_up, 3: x_dn}[pos]
        return remote(lacc.at[pos], lrecv.at[pos - 1], l_s.at[pos - 1], l_r.at[pos - 1], dev)

    def arrive(s, h):
        ty(s, h).wait_recv()
        tc(s, h).start()

    def arrive_sib(s, h):
        tc(s, h, receive=True).wait_recv()

    def pass_on(h):
        ty(2, h).start()
        if h + 2 < H:
            ty(1, h + 2).start()

    def hand_on_images():
        for d in range(2):
            ag(d, d).wait_recv()
            fw(d).start()

    def neighbours():
        for d in range(2):
            ag(d, 1 - d).wait_recv()

    def far():
        fw(0).wait_recv()
        fw(1).wait_recv()

    own_img.wait()
    for h in range(H):
        own_txt[h].wait()
    for h in range(H):
        tc(0, h, receive=True).wait_recv()
    far_match.wait_recv()
    own_scores(0)

    @pl.when(even)
    def _():
        arrive(1, 0)
        arrive(1, 1)
        arrive_sib(1, 0)
        arrive_sib(1, 1)
        scores_loop(1, lambda j: H + j, 2, lambda j: 0)
        arrive(1, 2)
        hand_on_images()
        neighbours()
        arrive(1, 3)
        scores_loop(2, lambda j: 0, H, lambda j: 2 + j)
        arrive_sib(1, 2)
        arrive_sib(1, 3)
        scores_loop(2, lambda j: H, H, lambda j: 2 + j)
        image_part(2, 0, 2 * H)
        direct_send(0, False)
        image_part(3, 0, 2 * H)
        direct_send(1, False)
        scores_loop(1, lambda j: H + 2 + j, 2, lambda j: 0)
        far()
        scores_loop(1, lambda j: H + j, H, lambda j: 1)
        text_part(1, 0, 2)
        text_part(1, 2, 2)
        q_send(1, 0)
        q_send(1, 1)
        own_scores(1)
        q_send(1, 2)
        q_send(1, 3)
        image_part(1, 0, 2 * H)
        rel_send()
        for pos in (1, 2, 3):
            loss_copy(pos).start()
        image_part(0, 0, 2 * H)
        text_part(0, 0, H)
        direct_send(0, True)
        direct_send(1, True)

    @pl.when(odd)
    def _():
        arrive(1, 0)
        pass_on(0)
        arrive(1, 1)
        pass_on(1)
        arrive_sib(1, 0)
        arrive_sib(1, 1)
        scores_loop(1, lambda j: H + j, 2, lambda j: 0)
        arrive(2, 0)
        hand_on_images()
        arrive_sib(2, 0)
        neighbours()
        scores_loop(2, lambda j: 2 * H, 1, lambda j: 2 + j)
        text_part(2, 0, 1, 2, 2)
        arrive(1, 2)
        pass_on(2)
        scores_loop(2, lambda j: H, 2, lambda j: 2 + j)
        q_send(2, 0)
        arrive(2, 1)
        arrive_sib(2, 1)
        scores_loop(2, lambda j: 2 * H + 1, 1, lambda j: 2 + j)
        text_part(2, 1, 1, 2, 2)
        far()
        own_scores(1)
        q_send(2, 1)
        arrive(1, 3)
        pass_on(3)
        arrive_sib(1, 2)
        arrive_sib(1, 3)
        scores_loop(1, lambda j: H + j, H, lambda j: 1)
        image_part(1, 0, 2 * H)
        rel_send()
        text_part(1, 0, 2)
        scores_loop(3, lambda j: H + 2, 2, lambda j: j + jnp.minimum(j, 1))
        arrive(2, 2)
        q_send(1, 0, chain=True)
        q_send(1, 1, chain=True)
        image_part(2, H, H)
        image_part(3, H, H)
        arrive(2, 3)
        text_part(1, 2, 2)
        arrive_sib(2, 2)
        arrive_sib(2, 3)
        scores_loop(2, lambda j: 2 * H + 2, 2, lambda j: 2 + j)
        image_part(2, 2 * H, H, add=True)
        direct_send(0, False)
        image_part(3, 2 * H, H, add=True)
        direct_send(1, False)
        text_part(2, 2, 2, 2, 2)
        for pos in (1, 2, 3):
            loss_copy(pos).start()
        image_part(0, 0, 2 * H)
        q_send(2, 2)
        q_send(2, 3)
        text_part(0, 0, H, 0, 2)
        q_send(1, 2, chain=True)
        direct_send(0, True)
        direct_send(1, True)
        q_send(1, 3, chain=True)

    for h in range(H):
        rows = pl.ds(text_row(0, h, core), SR)
        pt[rows, :] = chip_sum(0, h)
    q0_out = [
        pltpu.make_async_copy(pt.at[pl.ds(text_row(0, h, core), SR)], q0_o.at[pl.ds(h * SR, SR)], o_s.at[1 + h])
        for h in range(H)
    ]
    for h in range(H):
        q0_out[h].start()
    total = lacc[0]
    for pos in (1, 2, 3):
        loss_copy(pos).wait_recv()
        total = total + lrecv[pos - 1]
    loss_o[...] = total
    direct(0, 1).wait_recv()
    direct(1, 0).wait_recv()
    pi[pl.ds(0, B), :] += rx_pure[...].astype(jnp.float32)
    pi_out = pltpu.make_async_copy(pi.at[pl.ds(0, B)], pi_o, o_s.at[0])
    pi_out.start()

    for d in range(2):
        fw(d).wait_send()
        rel(d).wait_send()
        for half in range(2):
            ag(d, half).wait_send()
    for h in range(H):
        ty(1, h).wait_send()
        tc(0, h).wait_send()
        tc(1, h).wait_send()
        ex(0, h).wait_send()
        ex(1, h).wait_send()
    far_match.wait_send()
    for pos in (1, 2, 3):
        loss_copy(pos).wait_send()

    @pl.when(odd)
    def _():
        for h in range(H):
            ty(2, h).wait_send()
            tc(2, h).wait_send()
            ex(2, h).wait_send()
            q(2, h).wait_send()

    for h in range(H):
        q0_out[h].wait()
    pi_out.wait()
    for d in range(2):
        for half in range(2):
            direct(d, half).wait_send()
        direct(d, d).wait_recv()
    for h in range(H):
        q(1, h).wait()


def finish(scale, loss, pi, late, q0, ry, loss_o, di_o, dt_o):
    s = scale[0]
    di_o[...] = s * (pi[...] + late[...].astype(jnp.float32))
    dt_o[...] = s * (q0[...] + ry[...].astype(jnp.float32))
    loss_o[...] = LN2 * jnp.sum(loss[...], axis=0, keepdims=True)


def text_row(s, h, core):
    return pl.multiple_of(((s * H + h) * 2 + core) * SR, SR)


def body(pic, cap, mat, sc, sh):
    any_spec = pl.BlockSpec(memory_space=pl.ANY)
    vmem = pl.BlockSpec(memory_space=pltpu.VMEM)
    smem = pl.BlockSpec(memory_space=pltpu.SMEM)
    f32, bf16 = jnp.float32, jnp.bfloat16
    dma = pltpu.SemaphoreType.DMA
    parts = pl.pallas_call(
        kernel,
        name="band",
        out_shape=(
            jax.ShapeDtypeStruct((8, B), f32),
            jax.ShapeDtypeStruct((B, D), f32),
            jax.ShapeDtypeStruct((B, D), bf16),
            jax.ShapeDtypeStruct((B, D), f32),
            jax.ShapeDtypeStruct((B, D), bf16),
        ),
        in_specs=[any_spec] * 5,
        out_specs=(vmem, any_spec, any_spec, any_spec, any_spec),
        scratch_shapes=[
            pltpu.SMEM((2, 1), f32),
            pltpu.VMEM((4 * B, D), bf16),
            pltpu.VMEM((TILES * TR, D), bf16),
            pltpu.VMEM((TILES * TR, 4 * B), bf16),
            pltpu.VMEM((4 * B, TILES * TR), bf16),
            pltpu.VMEM((2, 1, B), jnp.int32),
            pltpu.VMEM((4, 8, B), f32),
            pltpu.VMEM((3, 8, B), f32),
            pltpu.VMEM((4 * B, D), f32),
            pltpu.VMEM((TILES * TR, D), f32),
            pltpu.VMEM((TILES * SR, D), f32),
            pltpu.VMEM((2 * B, D), bf16),
            pltpu.VMEM((B, D), bf16),
            pltpu.VMEM((B, D), bf16),
            pltpu.VMEM((B, D), bf16),
            pltpu.VMEM((2 * B, D), bf16),
            pltpu.VMEM((B, D), bf16),
            dma((4 + H,)),
            dma((2, 2)), dma((2, 2)),
            dma((2,)), dma((2,)),
            dma((2, H)), dma((2, H)),
            dma((3, H)), dma((3, H)),
            dma, dma,
            dma((2, 2)), dma((2, 2)),
            dma((2,)), dma((2,)),
            dma((2, H)), dma((2, H)),
            dma((3, H)), dma((3, H)),
            dma((3,)), dma((3,)),
            dma((1 + H,)),
        ],
        compiler_params=pltpu.CompilerParams(
            collective_id=0, has_side_effects=True, vmem_limit_bytes=56 * 2**20
        ),
        cost_estimate=pl.CostEstimate(flops=7247757312, bytes_accessed=3600000, transcendentals=3145728),
    )(pic, cap.reshape(H, SR, D), mat.reshape(1, B), sc, sh)
    blocks = 2
    rows = pl.BlockSpec((B // blocks, D), lambda i: (i, 0))
    loss, di, dt = pl.pallas_call(
        finish,
        name="finish",
        grid=(blocks,),
        out_shape=(
            jax.ShapeDtypeStruct((1, B), f32),
            jax.ShapeDtypeStruct((B, D), f32),
            jax.ShapeDtypeStruct((B, D), f32),
        ),
        in_specs=[smem, pl.BlockSpec((8, B), lambda i: (0, 0)), rows, rows, rows, rows],
        out_specs=(pl.BlockSpec((1, B), lambda i: (0, 0)), rows, rows),
    )(sc, *parts)
    return loss.reshape(B), di, dt


def solution(mesh):
    return jax.shard_map(
        body,
        mesh=mesh,
        in_specs=(P(("img", "txt"), None), P(("img", "txt"), None), P(("img", "txt")), P(), P()),
        out_specs=(P(("img", "txt")), P(("img", "txt"), None), P(("img", "txt"), None)),
        check_vma=False,
    )
```

time: 80 us -> 65.3 us (0.82)
  Pallas kernels: 73.2 us -> 63.1 us
  local copies, waits for them, and re-layouts: 4.71 us -> 0 us
    pallas_call x1 -> x2, Pallas kernels: 73.2 us -> 63.1 us  [the longest x1 60.1 us: body(): pl.pallas_call(kernel, name='band', out_shape=(jax.ShapeDtypeStruct((8, B...]
    unnamed x5 -> x0, local copies, waits for them, and re-layouts: 4.71 us -> none
where the time goes in v2:
time: 65.3 us; the launch traced here: 65.2 us
  Pallas kernels  63.1 us (97%)
  between operations  2.03 us (3%)
    pallas_call x1, Pallas kernels, body(): pl.pallas_call(kernel, name='band', out_shape=(jax.ShapeDtypeStruct((8, B...  60.1 us
    pallas_call x1, Pallas kernels, body(): pl.pallas_call(finish, name='finish', grid=(blocks,), out_shape=(jax.Shap...  3.07 us

profile of v2, /device:TPU:1, one launch (start us, length us, event | category | flops | bytes accessed | tf_op | source)
XLA Modules:
  0.0 65.2 jit_solution(7685182983961410179)
XLA Ops:
  1.9 60.1 %band.1 = (f32[8,256]{1,0:T(8,128)}, f32[256,1152]{1,0:T(8,128)}, bf16[256,1152]{1,0:T(8,128)(2,1)}, f32[256,1152]{1,0:T(8,128)}, bf16[256,1152]{1,0:T(8,128)(2,1)}) custom-call(bf16[256,1152]{1,0:T(8,128)(2,1)} %pic.1, bf16[4,64,1152]{2,1,0:T(8,128)(2,1)} %bitcast.3, s32[1,256]{1,0:T(1,128)} %bitcast.4, f32[1]{0:T(128)S(6)} %copy.8.sc.scale, f32[1]{0:T(128)S(6)} %copy.9.sh), custom_call_target="tpu_custom_call" | custom-call | flops 7247757312 | bytes 3600000 | tf_op jit(solution)/shard_map/band/pallas_call | solution.py:435
  62.0 3.1 %finish.1 = (f32[1,256]{1,0:T(1,128)}, f32[256,1152]{1,0:T(8,128)}, f32[256,1152]{1,0:T(8,128)}) custom-call(f32[1]{0:T(128)S(6)} %copy.8.sc.scale, f32[8,256]{1,0:T(8,128)} %get-tuple-element.11.loss, f32[256,1152]{1,0:T(8,128)} %get-tuple-element.12.pi, bf16[256,1152]{1,0:T(8,128)(2,1)} %get-tuple-element.13.late, f32[256,1152]{1,0:T(8,128)} %get-tuple-element.14.q0, ...), custom_call_target="tpu_custom_call" | custom-call | tf_op jit(solution)/shard_map/finish/pallas_call | solution.py:485

commit v3 on v2

--- a/solution.py
+++ b/solution.py
@@ -24,9 +24,10 @@
 def kernel(
     pic, cap, mat, sc, sh, loss_o, pi_o, rx_late, q0_o, ry_o,
     scal, img, txt, wt, wn, matm, lacc, lrecv, pi, pt, rcc,
-    sx_dir, rx_pure, sx_rel, rx_rel, sy_q, ry_q2,
+    sx_dir, rx_pure, sx_rel, rx_rel, sy_q, ry_q2, tr, tq, rq,
     lsem, ag_s, ag_r, fw_s, fw_r, ty_s, ty_r, tc_s, tc_r, m_s, m_r,
     dir_s, dir_r, rel_s, rel_r, q_s, q_r, ex_s, ex_r, l_s, l_r, o_s,
+    tr_s, tr_r, tf_s, tf_r, tq_s, tq_r, tg_s, tg_r,
 ):
     gi = lax.axis_index("img")
     ti = lax.axis_index("txt")
@@ -44,9 +45,20 @@
     y_up = ((gi + 2) % NIMG, ti)
     y_dn = ((gi + NIMG - 2) % NIMG, ti)
     sib = (gi, xhi * 2 + other)
+    y, z = (gi // 2) % 4, gi // 8
+    above, below = (y + 1) % 4, (y + 3) % 4
+
+    def at(yy, zz):
+        return ((zz + 8) % 8 * 8 + yy * 2 + xlo, ti)
+
+    far_up, far_dn = at(above, z), at(below, z)
+    hand_to, hand_from = at(below, z + above // 2), at(above, z - 1 + y // 2)
+    home_to, home_from = at(above, z - 1 + below // 2), at(below, z + 1 - ((y + 2) % 4) // 2)
 
     barrier = pltpu.get_barrier_semaphore()
-    for dev in (x_up, x_dn, x_far, y_up, y_dn, sib):
+    partners = (x_up, x_dn, x_far, y_up, y_dn, sib)
+    partners += (far_up, far_dn, hand_to, hand_from, home_to, home_from)
+    for dev in partners:
         pl.semaphore_signal(barrier, inc=1, device_id=dev, device_id_type=MESH)
 
     own_img = pltpu.make_async_copy(pic, img.at[pl.ds(0, B)], lsem.at[0])
@@ -65,7 +77,7 @@
     for copy in small:
         copy.start()
     lacc[...] = jnp.zeros_like(lacc)
-    pl.semaphore_wait(barrier, 6)
+    pl.semaphore_wait(barrier, len(partners))
 
     def remote(src, dst, s, r, dev):
         return pltpu.make_async_remote_copy(
@@ -96,21 +108,27 @@
         dst = txt.at[pl.ds(text_row(s, h, other if receive else core), SR)]
         return remote(src, dst, tc_s.at[s, h], tc_r.at[s, h], sib)
 
-    ty(1, 0).start()
+    def there(i):
+        return remote(cap.at[H // 2 + i], tr.at[pl.ds(i * SR, SR)], tr_s.at[i], tr_r.at[i], far_dn)
+
+    def onward(i):
+        dst = txt.at[pl.ds(text_row(2, H // 2 + i, core), SR)]
+        return remote(tr.at[pl.ds(i * SR, SR)], dst, tf_s.at[i], tf_r.at[i], hand_to)
+
     far_match = remote(mat, matm.at[1], m_s, m_r, x_far)
     far_match.start()
-    for h in range(H):
-        tc(0, h).start()
+    ty(1, 0).start()
+    pl.when(odd)(there(0).start)
     ag(0, 0).start()
     ag(1, 1).start()
+    pl.when(odd)(there(1).start)
+    for h in range(H):
+        tc(0, h).start()
     ty(1, 1).start()
     ag(0, 1).start()
     ag(1, 0).start()
-
-    @pl.when(even)
-    def _():
-        for h in range(2, H):
-            ty(1, h).start()
+    for h in range(2, H):
+        ty(1, h).start()
 
     for copy in small:
         copy.wait()
@@ -157,12 +175,11 @@
     def own_scores(pos):
         scores(0, H, pos, True)
 
-    def image_part(pos, tile, count, add=False):
+    def image_part(pos, tile, count):
         cols = pl.ds(tile * TR, count * TR)
-        part = jnp.dot(wn[pl.ds(pos * B, B), cols], txt[cols, :], preferred_element_type=jnp.float32)
-        if add:
-            part = part + pi[pl.ds(pos * B, B)]
-        pi[pl.ds(pos * B, B)] = part
+        pi[pl.ds(pos * B, B)] = jnp.dot(
+            wn[pl.ds(pos * B, B), cols], txt[cols, :], preferred_element_type=jnp.float32
+        )
 
     def text_part(s, h, count, first=0, blocks=4):
         rows = pl.ds((s * H + h) * TR, count * TR)
@@ -197,6 +214,22 @@
             value = value + ry_q2[pl.ds(h * SR, SR), :].astype(jnp.float32)
         sy_q[pl.ds(((s - 1) * H + h) * SR, SR), :] = value.astype(jnp.bfloat16)
         q(s, h).start()
+
+    def back(h):
+        rows = pl.ds(h * SR, SR)
+        return remote(sy_q.at[pl.ds((H + h) * SR, SR)], tq.at[rows], tq_s.at[h], tq_r.at[h], far_up)
+
+    def home(h):
+        rows = pl.ds(h * SR, SR)
+        return remote(tq.at[rows], rq.at[rows], tg_s.at[h], tg_r.at[h], home_to)
+
+    def back_send(h):
+        sy_q[pl.ds((H + h) * SR, SR), :] = chip_sum(2, h).astype(jnp.bfloat16)
+        back(h).start()
+
+    def home_send(h):
+        back(h).wait_recv()
+        home(h).start()
 
     def rel(d):
         rows = pl.ds(d * HALF, HALF)
@@ -230,16 +263,15 @@
         return remote(lacc.at[pos], lrecv.at[pos - 1], l_s.at[pos - 1], l_r.at[pos - 1], dev)
 
     def arrive(s, h):
-        ty(s, h).wait_recv()
+        (onward(h - H // 2) if s == 2 and h >= H // 2 else ty(s, h)).wait_recv()
         tc(s, h).start()
 
     def arrive_sib(s, h):
         tc(s, h, receive=True).wait_recv()
 
     def pass_on(h):
-        ty(2, h).start()
-        if h + 2 < H:
-            ty(1, h + 2).start()
+        there(h).wait_recv()
+        onward(h).start()
 
     def hand_on_images():
         for d in range(2):
@@ -266,11 +298,11 @@
     def _():
         arrive(1, 0)
         arrive(1, 1)
+        hand_on_images()
         arrive_sib(1, 0)
         arrive_sib(1, 1)
         scores_loop(1, lambda j: H + j, 2, lambda j: 0)
         arrive(1, 2)
-        hand_on_images()
         neighbours()
         arrive(1, 3)
         scores_loop(2, lambda j: 0, H, lambda j: 2 + j)
@@ -284,86 +316,96 @@
         scores_loop(1, lambda j: H + 2 + j, 2, lambda j: 0)
         far()
         scores_loop(1, lambda j: H + j, H, lambda j: 1)
+        own_scores(1)
+        image_part(1, 0, 2 * H)
+        rel_send()
         text_part(1, 0, 2)
+        for pos in (1, 2, 3):
+            loss_copy(pos).start()
         text_part(1, 2, 2)
         q_send(1, 0)
         q_send(1, 1)
-        own_scores(1)
+        text_part(0, 0, 2)
         q_send(1, 2)
         q_send(1, 3)
-        image_part(1, 0, 2 * H)
-        rel_send()
-        for pos in (1, 2, 3):
-            loss_copy(pos).start()
+        text_part(0, 2, 2)
         image_part(0, 0, 2 * H)
-        text_part(0, 0, H)
         direct_send(0, True)
         direct_send(1, True)
 
     @pl.when(odd)
     def _():
         arrive(1, 0)
-        pass_on(0)
+        ty(2, 0).start()
         arrive(1, 1)
-        pass_on(1)
+        ty(2, 1).start()
+        hand_on_images()
         arrive_sib(1, 0)
         arrive_sib(1, 1)
         scores_loop(1, lambda j: H + j, 2, lambda j: 0)
+        pass_on(0)
+        arrive(1, 2)
+        pass_on(1)
+        arrive(2, 2)
+        neighbours()
+        arrive(1, 3)
+        scores_loop(2, lambda j: H, 2, lambda j: 2 + j)
+        arrive_sib(1, 2)
+        arrive_sib(1, 3)
+        scores_loop(3, lambda j: H + 2, 2, lambda j: j + jnp.minimum(j, 1))
+        arrive(2, 3)
         arrive(2, 0)
-        hand_on_images()
-        arrive_sib(2, 0)
-        neighbours()
-        scores_loop(2, lambda j: 2 * H, 1, lambda j: 2 + j)
-        text_part(2, 0, 1, 2, 2)
-        arrive(1, 2)
-        pass_on(2)
-        scores_loop(2, lambda j: H, 2, lambda j: 2 + j)
-        q_send(2, 0)
-        arrive(2, 1)
-        arrive_sib(2, 1)
-        scores_loop(2, lambda j: 2 * H + 1, 1, lambda j: 2 + j)
-        text_part(2, 1, 1, 2, 2)
+        arrive_sib(2, 2)
+        scores_loop(2, lambda j: 2 * H + 2, 1, lambda j: 2 + j)
+        text_part(2, 2, 1, 2, 2)
         far()
         own_scores(1)
-        q_send(2, 1)
-        arrive(1, 3)
-        pass_on(3)
-        arrive_sib(1, 2)
-        arrive_sib(1, 3)
+        q_send(2, 2)
+        arrive(2, 1)
         scores_loop(1, lambda j: H + j, H, lambda j: 1)
         image_part(1, 0, 2 * H)
         rel_send()
         text_part(1, 0, 2)
-        scores_loop(3, lambda j: H + 2, 2, lambda j: j + jnp.minimum(j, 1))
-        arrive(2, 2)
-        q_send(1, 0, chain=True)
-        q_send(1, 1, chain=True)
-        image_part(2, H, H)
-        image_part(3, H, H)
-        arrive(2, 3)
+        arrive_sib(2, 3)
+        scores_loop(2, lambda j: 2 * H + 3, 1, lambda j: 2 + j)
+        arrive_sib(2, 0)
+        arrive_sib(2, 1)
+        q_send(1, 0)
+        scores_loop(2, lambda j: 2 * H, 2, lambda j: 2 + j)
+        q_send(1, 1)
+        text_part(2, 0, 2, 2, 2)
+        image_part(2, H, 2 * H)
+        direct_send(0, False)
+        back_send(0)
+        back_send(1)
+        image_part(3, H, 2 * H)
+        direct_send(1, False)
+        text_part(2, 3, 1, 2, 2)
         text_part(1, 2, 2)
-        arrive_sib(2, 2)
-        arrive_sib(2, 3)
-        scores_loop(2, lambda j: 2 * H + 2, 2, lambda j: 2 + j)
-        image_part(2, 2 * H, H, add=True)
-        direct_send(0, False)
-        image_part(3, 2 * H, H, add=True)
-        direct_send(1, False)
-        text_part(2, 2, 2, 2, 2)
+        q_send(2, 3)
         for pos in (1, 2, 3):
             loss_copy(pos).start()
         image_part(0, 0, 2 * H)
-        q_send(2, 2)
-        q_send(2, 3)
-        text_part(0, 0, H, 0, 2)
+        text_part(0, 0, 2, 0, 2)
+        text_part(0, 2, 2, 0, 2)
         q_send(1, 2, chain=True)
+        home_send(0)
         direct_send(0, True)
         direct_send(1, True)
+        home_send(1)
         q_send(1, 3, chain=True)
 
     for h in range(H):
         rows = pl.ds(text_row(0, h, core), SR)
         pt[rows, :] = chip_sum(0, h)
+
+    @pl.when(odd)
+    def _():
+        for h in range(H // 2):
+            rows = pl.ds(text_row(0, h, core), SR)
+            home(h).wait_recv()
+            pt[rows, :] += rq[pl.ds(h * SR, SR), :].astype(jnp.float32)
+
     q0_out = [
         pltpu.make_async_copy(pt.at[pl.ds(text_row(0, h, core), SR)], q0_o.at[pl.ds(h * SR, SR)], o_s.at[1 + h])
         for h in range(H)
@@ -399,10 +441,15 @@
     @pl.when(odd)
     def _():
         for h in range(H):
-            ty(2, h).wait_send()
             tc(2, h).wait_send()
             ex(2, h).wait_send()
-            q(2, h).wait_send()
+        for h in range(H // 2):
+            ty(2, h).wait_send()
+            there(h).wait_send()
+            onward(h).wait_send()
+            q(2, H // 2 + h).wait_send()
+            back(h).wait_send()
+            home(h).wait_send()
 
     for h in range(H):
         q0_out[h].wait()
@@ -462,6 +509,9 @@
             pltpu.VMEM((B, D), bf16),
             pltpu.VMEM((2 * B, D), bf16),
             pltpu.VMEM((B, D), bf16),
+            pltpu.VMEM((B // 2, D), bf16),
+            pltpu.VMEM((B // 2, D), bf16),
+            pltpu.VMEM((B // 2, D), bf16),
             dma((4 + H,)),
             dma((2, 2)), dma((2, 2)),
             dma((2,)), dma((2,)),
@@ -474,6 +524,10 @@
             dma((3, H)), dma((3, H)),
             dma((3,)), dma((3,)),
             dma((1 + H,)),
+            dma((H // 2,)), dma((H // 2,)),
+            dma((H // 2,)), dma((H // 2,)),
+            dma((H // 2,)), dma((H // 2,)),
+            dma((H // 2,)), dma((H // 2,)),
         ],
         compiler_params=pltpu.CompilerParams(
             collective_id=0, has_side_effects=True, vmem_limit_bytes=56 * 2**20

time: 65.3 us -> 64.7 us (level); the launches traced: 65.2 us -> 63.6 us
  Pallas kernels: 63.1 us -> 61.6 us
    pallas_call x1, Pallas kernels: 60.1 us -> 58.5 us  [body(): pl.pallas_call(kernel, name='band', out_shape=(jax.ShapeDtypeStruct((8, B...]
where the time goes in v3:
time: 64.7 us; the launch traced here: 63.6 us
  Pallas kernels  61.6 us (95%)
  between operations  2.03 us (3%)
    pallas_call x1, Pallas kernels, body(): pl.pallas_call(kernel, name='band', out_shape=(jax.ShapeDtypeStruct((8, B...  58.5 us
    pallas_call x1, Pallas kernels, body(): pl.pallas_call(finish, name='finish', grid=(blocks,), out_shape=(jax.Shap...  3.07 us

profile of v3, /device:TPU:1, one launch (start us, length us, event | category | flops | bytes accessed | tf_op | source)
XLA Modules:
  0.0 63.6 jit_solution(14462361380467963452)
XLA Ops:
  1.9 58.5 %band.1 = (f32[8,256]{1,0:T(8,128)}, f32[256,1152]{1,0:T(8,128)}, bf16[256,1152]{1,0:T(8,128)(2,1)}, f32[256,1152]{1,0:T(8,128)}, bf16[256,1152]{1,0:T(8,128)(2,1)}) custom-call(bf16[256,1152]{1,0:T(8,128)(2,1)} %pic.1, bf16[4,64,1152]{2,1,0:T(8,128)(2,1)} %bitcast.3, s32[1,256]{1,0:T(1,128)} %bitcast.4, f32[1]{0:T(128)S(6)} %copy.8.sc.scale, f32[1]{0:T(128)S(6)} %copy.9.sh), custom_call_target="tpu_custom_call" | custom-call | flops 7247757312 | bytes 3600000 | tf_op jit(solution)/shard_map/band/pallas_call | solution.py:482
  60.4 3.1 %finish.1 = (f32[1,256]{1,0:T(1,128)}, f32[256,1152]{1,0:T(8,128)}, f32[256,1152]{1,0:T(8,128)}) custom-call(f32[1]{0:T(128)S(6)} %copy.8.sc.scale, f32[8,256]{1,0:T(8,128)} %get-tuple-element.11.loss, f32[256,1152]{1,0:T(8,128)} %get-tuple-element.12.pi, bf16[256,1152]{1,0:T(8,128)(2,1)} %get-tuple-element.13.late, f32[256,1152]{1,0:T(8,128)} %get-tuple-element.14.q0, ...), custom_call_target="tpu_custom_call" | custom-call | tf_op jit(solution)/shard_map/finish/pallas_call | solution.py:539

commit v4 on v3

--- a/solution.py
+++ b/solution.py
@@ -24,7 +24,7 @@
 def kernel(
     pic, cap, mat, sc, sh, loss_o, pi_o, rx_late, q0_o, ry_o,
     scal, img, txt, wt, wn, matm, lacc, lrecv, pi, pt, rcc,
-    sx_dir, rx_pure, sx_rel, rx_rel, sy_q, ry_q2, tr, tq, rq,
+    sx_dir, rx_pure, sx_rel, rx_rel, sy_q, ry_q2, tr, tq, rq, lout,
     lsem, ag_s, ag_r, fw_s, fw_r, ty_s, ty_r, tc_s, tc_r, m_s, m_r,
     dir_s, dir_r, rel_s, rel_r, q_s, q_r, ex_s, ex_r, l_s, l_r, o_s,
     tr_s, tr_r, tf_s, tf_r, tq_s, tq_r, tg_s, tg_r,
@@ -136,7 +136,7 @@
     shift = scal[1, 0] * LOG2E
     text_base = gi * 1024 + xhi * 512
 
-    def scores(tile, count, pos, labelled):
+    def scores(tile, count, pos, labelled, has_label=None):
         n = count * TR
         rows = pl.ds(pl.multiple_of(tile * TR, TR), n)
         images = pl.ds(pl.multiple_of(pos * B, B), B)
@@ -155,6 +155,8 @@
         if labelled:
             i = lax.broadcasted_iota(jnp.int32, (n, 1), 0)
             ids = text_base + ((i % TR) // SR) * B + (i // TR) * SR + i % SR
+            if has_label is not None:
+                ids = jnp.where(has_label, ids, -1)
             label = ids == matm[pos]
             w = jnp.where(jnp.logical_xor(positive, label), big, small)
             w = jnp.where(label, -w, w)
@@ -174,6 +176,11 @@
 
     def own_scores(pos):
         scores(0, H, pos, True)
+
+    def far_scores():
+        @pl.loop(0, 2)
+        def _(j):
+            scores(j * H, H, 1, True, j == 0)
 
     def image_part(pos, tile, count):
         cols = pl.ds(tile * TR, count * TR)
@@ -315,8 +322,7 @@
         direct_send(1, False)
         scores_loop(1, lambda j: H + 2 + j, 2, lambda j: 0)
         far()
-        scores_loop(1, lambda j: H + j, H, lambda j: 1)
-        own_scores(1)
+        far_scores()
         image_part(1, 0, 2 * H)
         rel_send()
         text_part(1, 0, 2)
@@ -359,25 +365,24 @@
         scores_loop(2, lambda j: 2 * H + 2, 1, lambda j: 2 + j)
         text_part(2, 2, 1, 2, 2)
         far()
-        own_scores(1)
+        far_scores()
         q_send(2, 2)
         arrive(2, 1)
-        scores_loop(1, lambda j: H + j, H, lambda j: 1)
         image_part(1, 0, 2 * H)
         rel_send()
         text_part(1, 0, 2)
+        arrive_sib(2, 0)
+        arrive_sib(2, 1)
+        scores_loop(2, lambda j: 2 * H, 2, lambda j: 2 + j)
+        q_send(1, 0)
+        text_part(2, 0, 2, 2, 2)
+        q_send(1, 1)
         arrive_sib(2, 3)
         scores_loop(2, lambda j: 2 * H + 3, 1, lambda j: 2 + j)
-        arrive_sib(2, 0)
-        arrive_sib(2, 1)
-        q_send(1, 0)
-        scores_loop(2, lambda j: 2 * H, 2, lambda j: 2 + j)
-        q_send(1, 1)
-        text_part(2, 0, 2, 2, 2)
+        back_send(0)
+        back_send(1)
         image_part(2, H, 2 * H)
         direct_send(0, False)
-        back_send(0)
-        back_send(1)
         image_part(3, H, 2 * H)
         direct_send(1, False)
         text_part(2, 3, 1, 2, 2)
@@ -392,36 +397,38 @@
         home_send(0)
         direct_send(0, True)
         direct_send(1, True)
+        q_send(1, 3, chain=True)
         home_send(1)
-        q_send(1, 3, chain=True)
-
-    for h in range(H):
-        rows = pl.ds(text_row(0, h, core), SR)
-        pt[rows, :] = chip_sum(0, h)
-
-    @pl.when(odd)
-    def _():
-        for h in range(H // 2):
-            rows = pl.ds(text_row(0, h, core), SR)
-            home(h).wait_recv()
-            pt[rows, :] += rq[pl.ds(h * SR, SR), :].astype(jnp.float32)
-
-    q0_out = [
-        pltpu.make_async_copy(pt.at[pl.ds(text_row(0, h, core), SR)], q0_o.at[pl.ds(h * SR, SR)], o_s.at[1 + h])
-        for h in range(H)
-    ]
-    for h in range(H):
-        q0_out[h].start()
-    total = lacc[0]
+
     for pos in (1, 2, 3):
         loss_copy(pos).wait_recv()
-        total = total + lrecv[pos - 1]
-    loss_o[...] = total
+    lout[pl.ds(0, 8), :] = lacc[0] + lrecv[0] + lrecv[1] + lrecv[2]
+    lout[pl.ds(8, 8), :] = jnp.full((8, B), scal[0, 0], jnp.float32)
+    loss_out = pltpu.make_async_copy(lout, loss_o, o_s.at[1 + H])
+    loss_out.start()
+
+    def q0_out(h):
+        rows = pl.ds(text_row(0, h, core), SR)
+        return pltpu.make_async_copy(pt.at[rows], q0_o.at[pl.ds(h * SR, SR)], o_s.at[1 + h])
+
+    for h in range(H // 2, H):
+        pt[pl.ds(text_row(0, h, core), SR), :] = chip_sum(0, h)
+        q0_out(h).start()
     direct(0, 1).wait_recv()
     direct(1, 0).wait_recv()
     pi[pl.ds(0, B), :] += rx_pure[...].astype(jnp.float32)
     pi_out = pltpu.make_async_copy(pi.at[pl.ds(0, B)], pi_o, o_s.at[0])
     pi_out.start()
+    for h in range(H // 2):
+        rows = pl.ds(text_row(0, h, core), SR)
+        pt[rows, :] = chip_sum(0, h)
+
+        @pl.when(odd)
+        def _():
+            home(h).wait_recv()
+            pt[rows, :] += rq[pl.ds(h * SR, SR), :].astype(jnp.float32)
+
+        q0_out(h).start()
 
     for d in range(2):
         fw(d).wait_send()
@@ -452,8 +459,9 @@
             home(h).wait_send()
 
     for h in range(H):
-        q0_out[h].wait()
+        q0_out(h).wait()
     pi_out.wait()
+    loss_out.wait()
     for d in range(2):
         for half in range(2):
             direct(d, half).wait_send()
@@ -462,11 +470,11 @@
         q(1, h).wait()
 
 
-def finish(scale, loss, pi, late, q0, ry, loss_o, di_o, dt_o):
-    s = scale[0]
+def finish(loss, pi, late, q0, ry, loss_o, di_o, dt_o):
+    s = loss[8:9, 0:1]
     di_o[...] = s * (pi[...] + late[...].astype(jnp.float32))
     dt_o[...] = s * (q0[...] + ry[...].astype(jnp.float32))
-    loss_o[...] = LN2 * jnp.sum(loss[...], axis=0, keepdims=True)
+    loss_o[...] = LN2 * jnp.sum(loss[0:8, :], axis=0, keepdims=True)
 
 
 def text_row(s, h, core):
@@ -475,22 +483,21 @@
 
 def body(pic, cap, mat, sc, sh):
     any_spec = pl.BlockSpec(memory_space=pl.ANY)
-    vmem = pl.BlockSpec(memory_space=pltpu.VMEM)
-    smem = pl.BlockSpec(memory_space=pltpu.SMEM)
+    hbm = pl.BlockSpec(memory_space=pltpu.HBM)
     f32, bf16 = jnp.float32, jnp.bfloat16
     dma = pltpu.SemaphoreType.DMA
     parts = pl.pallas_call(
         kernel,
         name="band",
         out_shape=(
-            jax.ShapeDtypeStruct((8, B), f32),
+            jax.ShapeDtypeStruct((16, B), f32),
             jax.ShapeDtypeStruct((B, D), f32),
             jax.ShapeDtypeStruct((B, D), bf16),
             jax.ShapeDtypeStruct((B, D), f32),
             jax.ShapeDtypeStruct((B, D), bf16),
         ),
-        in_specs=[any_spec] * 5,
-        out_specs=(vmem, any_spec, any_spec, any_spec, any_spec),
+        in_specs=[any_spec] * 3 + [hbm] * 2,
+        out_specs=(any_spec,) * 5,
         scratch_shapes=[
             pltpu.SMEM((2, 1), f32),
             pltpu.VMEM((4 * B, D), bf16),
@@ -512,6 +519,7 @@
             pltpu.VMEM((B // 2, D), bf16),
             pltpu.VMEM((B // 2, D), bf16),
             pltpu.VMEM((B // 2, D), bf16),
+            pltpu.VMEM((16, B), f32),
             dma((4 + H,)),
             dma((2, 2)), dma((2, 2)),
             dma((2,)), dma((2,)),
@@ -523,7 +531,7 @@
             dma((2, H)), dma((2, H)),
             dma((3, H)), dma((3, H)),
             dma((3,)), dma((3,)),
-            dma((1 + H,)),
+            dma((2 + H,)),
             dma((H // 2,)), dma((H // 2,)),
             dma((H // 2,)), dma((H // 2,)),
             dma((H // 2,)), dma((H // 2,)),
@@ -545,9 +553,9 @@
             jax.ShapeDtypeStruct((B, D), f32),
             jax.ShapeDtypeStruct((B, D), f32),
         ),
-        in_specs=[smem, pl.BlockSpec((8, B), lambda i: (0, 0)), rows, rows, rows, rows],
+        in_specs=[pl.BlockSpec((16, B), lambda i: (0, 0)), rows, rows, rows, rows],
         out_specs=(pl.BlockSpec((1, B), lambda i: (0, 0)), rows, rows),
-    )(sc, *parts)
+    )(*parts)
     return loss.reshape(B), di, dt
 
 

time: 64.7 us -> 62.7 us (0.969); the launches traced: 63.6 us -> 62.6 us
  Pallas kernels: 61.6 us -> 60.5 us
    pallas_call x1, Pallas kernels: 58.5 us -> 57.4 us  [body(): pl.pallas_call(kernel, name='band', out_shape=(jax.ShapeDtypeStruct((16,...]
where the time goes in v4:
time: 62.7 us; the launch traced here: 62.6 us
  Pallas kernels  60.5 us (96%)
  between operations  2.03 us (3%)
    pallas_call x1, Pallas kernels, body(): pl.pallas_call(kernel, name='band', out_shape=(jax.ShapeDtypeStruct((16,...  57.4 us
    pallas_call x1, Pallas kernels, body(): pl.pallas_call(finish, name='finish', grid=(blocks,), out_shape=(jax.Shap...  3.11 us

profile of v4, /device:TPU:1, one launch (start us, length us, event | category | flops | bytes accessed | tf_op | source)
XLA Modules:
  0.0 62.6 jit_solution(14368775870121084464)
XLA Ops:
  1.9 57.4 %band.1 = (f32[16,256]{1,0:T(8,128)}, f32[256,1152]{1,0:T(8,128)}, bf16[256,1152]{1,0:T(8,128)(2,1)}, f32[256,1152]{1,0:T(8,128)}, bf16[256,1152]{1,0:T(8,128)(2,1)}) custom-call(bf16[256,1152]{1,0:T(8,128)(2,1)} %pic.1, bf16[4,64,1152]{2,1,0:T(8,128)(2,1)} %bitcast.3, s32[1,256]{1,0:T(1,128)} %bitcast.4, f32[1]{0:T(128)S(6)} %copy.8.sc, f32[1]{0:T(128)S(6)} %copy.9.sh), custom_call_target="tpu_custom_call" | custom-call | flops 7247757312 | bytes 3600000 | tf_op jit(solution)/shard_map/band/pallas_call | solution.py:489
  59.3 3.1 %finish.1 = (f32[1,256]{1,0:T(1,128)}, f32[256,1152]{1,0:T(8,128)}, f32[256,1152]{1,0:T(8,128)}) custom-call(f32[16,256]{1,0:T(8,128)} %get-tuple-element.11.loss, f32[256,1152]{1,0:T(8,128)} %get-tuple-element.12.pi, bf16[256,1152]{1,0:T(8,128)(2,1)} %get-tuple-element.13.late, f32[256,1152]{1,0:T(8,128)} %get-tuple-element.14.q0, ...), custom_call_target="tpu_custom_call" | custom-call | tf_op jit(solution)/shard_map/finish/pallas_call | solution.py:547

commit v5 on v4

--- a/solution.py
+++ b/solution.py
@@ -317,14 +317,14 @@
         arrive_sib(1, 3)
         scores_loop(2, lambda j: H, H, lambda j: 2 + j)
         image_part(2, 0, 2 * H)
-        direct_send(0, False)
         image_part(3, 0, 2 * H)
-        direct_send(1, False)
         scores_loop(1, lambda j: H + 2 + j, 2, lambda j: 0)
         far()
         far_scores()
         image_part(1, 0, 2 * H)
         rel_send()
+        direct_send(0, False)
+        direct_send(1, False)
         text_part(1, 0, 2)
         for pos in (1, 2, 3):
             loss_copy(pos).start()
@@ -370,17 +370,17 @@
         arrive(2, 1)
         image_part(1, 0, 2 * H)
         rel_send()
-        text_part(1, 0, 2)
         arrive_sib(2, 0)
         arrive_sib(2, 1)
         scores_loop(2, lambda j: 2 * H, 2, lambda j: 2 + j)
-        q_send(1, 0)
         text_part(2, 0, 2, 2, 2)
-        q_send(1, 1)
+        text_part(1, 0, 2)
+        back_send(0)
+        back_send(1)
         arrive_sib(2, 3)
         scores_loop(2, lambda j: 2 * H + 3, 1, lambda j: 2 + j)
-        back_send(0)
-        back_send(1)
+        q_send(1, 0)
+        q_send(1, 1)
         image_part(2, H, 2 * H)
         direct_send(0, False)
         image_part(3, H, 2 * H)

time: 62.7 us -> 62.7 us (level)
  no operation moved by 1% of the time
where the time goes in v5:
time: 62.7 us; the launch traced here: 62.6 us
  Pallas kernels  60.5 us (96%)
  between operations  2.03 us (3%)
    pallas_call x1, Pallas kernels, body(): pl.pallas_call(kernel, name='band', out_shape=(jax.ShapeDtypeStruct((16,...  57.4 us
    pallas_call x1, Pallas kernels, body(): pl.pallas_call(finish, name='finish', grid=(blocks,), out_shape=(jax.Shap...  3.11 us

profile of v5, /device:TPU:1, one launch (start us, length us, event | category | flops | bytes accessed | tf_op | source)
XLA Modules:
  0.0 62.6 jit_solution(12589031257886693520)
XLA Ops:
  1.9 57.4 %band.1 = (f32[16,256]{1,0:T(8,128)}, f32[256,1152]{1,0:T(8,128)}, bf16[256,1152]{1,0:T(8,128)(2,1)}, f32[256,1152]{1,0:T(8,128)}, bf16[256,1152]{1,0:T(8,128)(2,1)}) custom-call(bf16[256,1152]{1,0:T(8,128)(2,1)} %pic.1, bf16[4,64,1152]{2,1,0:T(8,128)(2,1)} %bitcast.3, s32[1,256]{1,0:T(1,128)} %bitcast.4, f32[1]{0:T(128)S(6)} %copy.8.sc, f32[1]{0:T(128)S(6)} %copy.9.sh), custom_call_target="tpu_custom_call" | custom-call | flops 7247757312 | bytes 3600000 | tf_op jit(solution)/shard_map/band/pallas_call | solution.py:489
  59.3 3.1 %finish.1 = (f32[1,256]{1,0:T(1,128)}, f32[256,1152]{1,0:T(8,128)}, f32[256,1152]{1,0:T(8,128)}) custom-call(f32[16,256]{1,0:T(8,128)} %get-tuple-element.11.loss, f32[256,1152]{1,0:T(8,128)} %get-tuple-element.12.pi, bf16[256,1152]{1,0:T(8,128)(2,1)} %get-tuple-element.13.late, f32[256,1152]{1,0:T(8,128)} %get-tuple-element.14.q0, ...), custom_call_target="tpu_custom_call" | custom-call | tf_op jit(solution)/shard_map/finish/pallas_call | solution.py:547
